TPU v7x, 32 devices: a whole 2x2x4 slice. The times are simulated.
32 devices in a mesh: person: 4 (over z), var: 8 (over y, x, core).
Axes of the slice: x: 2, y: 2, z: 4, core: 2. Of those that a mesh axis runs over, the one named last changes fastest.
Arguments:
- linear_pred: float32 [64, 12288], P('var', 'person'), may hold values from -3 to 3
- event_flag: int32 [12288], P('person'), may hold values 0 or 1
- fold_id: int32 [12288], P('person'), may hold values from 0 to 7
- tie_group: int32 [12288], P('person'), may hold values from 0 to 12287, as said below
- time_order: int32 [12288], P('person'), may hold values from 0 to 12287, as said below
- genotypes: int32 [2048, 16384], P('person', 'var'), may hold values from 0 to 728, as said below
- variant_scale: float32 [16384], P('var'), may hold values from 1 to 4
- penalty: float32 [64], P('person'), may hold values from 0.3 to 3
- strong_set: int32 [64, 16384], P('person', 'var'), may hold values 0 or 1
Outputs:
- gradient: float32 [64, 16384], P('person', 'var')
- violation: float32 [64, 16384], P('person', 'var')
Inputs may be any that keep to these rules, and one draw needn't show every extreme that they name: `time_order`: A permutation. Each aligned block of 3072 consecutive event-time ranks holds exactly 768 persons of each aligned block of 3072 file positions. `tie_group`: never falls along event-time rank; each group is consecutive ranks inside one aligned block of 3072 ranks, holds at most 4 persons, and some group of every block holds exactly 4. `genotypes`: word r of a variant holds the allele counts (0, 1 or 2) of file persons 6 r to 6 r + 5 as base-3 digits, person 6 r + s with weight 3 ** s.
All inputs are finite; a program needn't handle non-finite values. No bound on the sum of `event_flag` or of `strong_set` on one device may be relied on, other than what follows from the above.
Results may differ from a plain program's by a relative error of at most 0.0036.
The roundings to bfloat16 on the way count: a program that leaves them out, or rounds other values in their place, can miss the bound.
Values may be sent and summed in bfloat16 or wider, within the bound.
A program may use at most 64 MiB of HBM per device.

v0:
```python
import math

import jax
import jax.numpy as jnp
from jax import lax
from jax.sharding import PartitionSpec as P

FOLDS = 8
TIE_MAX = 4


def carried_in(x, axis, combine, identity, reverse):
    size, place = (lax.axis_size(axis), lax.axis_index(axis))
    everything = lax.all_gather(x, axis)
    start = jnp.broadcast_to(jnp.asarray(identity, x.dtype), x.shape)

    def turn(k, before):
        at = size - 1 - k if reverse else k
        reached = at > place if reverse else at < place
        new = combine(before, everything[at])
        return jnp.where(reached, new, before)

    return lax.fori_loop(0, size, turn, start)


def add_pair(earlier, later):
    return earlier + later


def across_devices(totals, reverse):
    if reverse:
        return carried_in(totals, "person", add_pair, jnp.zeros_like(totals), True)
    return carried_in(totals, "person", add_pair, jnp.zeros_like(totals), False)


def group_first(values, tie_group):
    result = values
    for offset in range(1, TIE_MAX):
        moved = jnp.pad(values, ((0, 0), (offset, 0)))[:, :-offset]
        moved_tie = jnp.pad(tie_group, (offset, 0), constant_values=-1)[:-offset]
        result = jnp.maximum(result, jnp.where((moved_tie == tie_group)[None, :], moved, 0.0))
    return result


def group_last(values, tie_group):
    result = values
    for offset in range(1, TIE_MAX):
        moved = jnp.pad(values, ((0, 0), (0, offset)))[:, offset:]
        moved_tie = jnp.pad(tie_group, (0, offset), constant_values=-1)[offset:]
        result = jnp.maximum(result, jnp.where((moved_tie == tie_group)[None, :], moved, 0.0))
    return result


def residuals(linear_pred, event_flag, fold_id, tie_group, first_column):
    columns = first_column + jnp.arange(linear_pred.shape[0])
    weight = (fold_id[None, :] != (columns % FOLDS)[:, None]).astype(jnp.float32)
    events = event_flag.astype(jnp.float32)[None, :]
    risk = jnp.exp(linear_pred)
    suffix = lax.cumsum(weight * risk, axis=1, reverse=True)
    suffix = suffix + across_devices(suffix[:, 0], True)[:, None]
    at_risk = group_first(suffix, tie_group)
    hazard = weight * events / (at_risk + 1.0 - weight)
    prefix = jnp.cumsum(hazard, axis=1)
    prefix = prefix + across_devices(prefix[:, -1], False)[:, None]
    cumulative = group_last(prefix, tie_group)
    return (weight * (events - risk * cumulative)).astype(jnp.bfloat16)


def regroup(resid, file_index):
    width = resid.shape[1]
    target = file_index // width
    order = jnp.argsort(target, stable=True)
    ordered = jnp.take(resid, order, axis=1)
    place = jnp.take(file_index % width, order)
    digits = jnp.stack([place // 128, place % 128]).astype(jnp.bfloat16)
    arrived, labels = (
        lax.all_to_all(ordered, "person", split_axis=1, concat_axis=1, tiled=True),
        lax.all_to_all(digits, "person", split_axis=1, concat_axis=1, tiled=True),
    )
    slots = labels[0].astype(jnp.int32) * 128 + labels[1].astype(jnp.int32)
    return jnp.zeros_like(resid).at[:, slots].set(arrived)


def per_device(
    linear_pred,
    event_flag,
    fold_id,
    tie_group,
    time_order,
    genotypes,
    variant_scale,
    penalty,
    strong_set,
):
    persons = linear_pred.shape[1]
    first_column = lax.axis_index("var") * linear_pred.shape[0]
    own_resid = residuals(linear_pred, event_flag, fold_id, tie_group, first_column)
    in_file = lax.all_gather(regroup(own_resid, time_order), "var", axis=0, tiled=True)
    words = genotypes.shape[0]
    columns = in_file.shape[0]
    by_member = in_file.reshape(columns, words, 6)
    scores = jnp.zeros((columns, genotypes.shape[1]), jnp.float32)
    for member in range(6):
        dosage = (genotypes // 3**member % 3).astype(jnp.bfloat16)
        scores = scores + jnp.dot(
            by_member[:, :, member], dosage, preferred_element_type=jnp.float32
        )
    share = columns // lax.axis_size("person")
    summed = lax.psum(scores, "person")
    mine = lax.dynamic_slice_in_dim(summed, lax.axis_index("person") * share, share, 0)
    total_persons = persons * lax.axis_size("person")
    gradient = mine * variant_scale[None, :] / math.sqrt(total_persons)
    violation = (1 - strong_set).astype(jnp.float32) * jnp.maximum(
        jnp.abs(gradient) - penalty[:, None], 0.0
    )
    return (gradient, violation)


def solution(mesh):
    placed = (
        P("var", "person"),
        P("person"),
        P("person"),
        P("person"),
        P("person"),
        P("person", "var"),
        P("var"),
        P("person"),
        P("person", "var"),
    )
    return jax.shard_map(
        per_device,
        mesh=mesh,
        in_specs=placed,
        out_specs=(P("person", "var"), P("person", "var")),
        check_vma=False,
    )
```

profile of v0, /device:TPU:0, one launch (start us, length us, event | category | flops | bytes accessed | tf_op | source)
XLA Modules:
  0.0 206.1 jit_solution(1780009143035342721)
XLA Ops:
  7.9 5.8 %sort.17 = (s32[3072]{0:T(1024)}, s32[3072]{0:T(1024)S(1)}) sort(s32[3072]{0:T(1024)S(1)} %get-tuple-element.257, s32[3072]{0:T(1024)S(1)} %iota.9), dimensions={0}, to_apply=%region_0.1 | sort | flops 36864 | bytes 49152 | tf_op jit(solution)/shard_map/jit(argsort)/sort | solution.py:72
  13.7 17.4 %gather_fusion = s32[3072]{0:T(1024)S(1)} fusion(s32[3072]{0:T(1024)S(1)} %get-tuple-element.258, s32[3072]{0:T(1024)S(1)} %fusion.60), kind=kCustom, calls=%fused_computation | custom fusion | bytes 36864 | tf_op jit(solution)/shard_map/jit(_take)/gather | solution.py:74
  31.8 6.3 %all-to-all-start = ((bf16[2,4,768]{2,0,1:T(2,128)(2,1)}), bf16[2,4,768]{2,0,1:T(2,128)(2,1)S(1)}, u32[]{:S(2)}, u32[]{:S(2)}) async-start(bf16[2,4,768]{2,0,1:T(2,128)(2,1)} %copy.50), calls=%async_computation | async-start | bytes 24576 | tf_op jit(solution)/shard_map/all_to_all | solution.py:78
  38.7 1.4 compare_select_fusion.1
  40.5 10.0 %reduce-window.14 = f32[8,24,128]{2,1,0:T(8,128)S(1)} reduce-window(f32[8,24,128]{2,1,0:T(8,128)S(1)} %copy.52, f32[]{:T(128)} %constant.235.clone.1), window={size=1x1x128 pad=0_0x0_0x0_127}, to_apply=%region_1.2 | reduce-window | flops 3121152 | bytes 196612 | tf_op jit(solution)/shard_map/reduce-window
  52.8 12.2 %all-reduce.12 = f32[32]{0:T(128)S(1)} all-reduce(f32[32]{0:T(128)S(1)} %fusion.63), channel_id=2, replica_groups=mesh['person'=4,'var'=8] {'person'}, use_global_device_ids=true, to_apply=%add.12 | all-reduce | flops 32 | bytes 256
  65.5 3.1 %fusion.28 = f32[8,3072]{0,1:T(8,128)S(1)} fusion(f32[8,3072]{0,1:T(8,128)S(1)} %broadcast_add_fusion.1, f32[3072]{0:T(1024)S(1)} %convert_element_type.68, s32[8]{0:T(128)S(1)} %and_select_fusion, s32[3072]{0:T(1024)S(1)} %copy-done.1, pred[3072]{0:T(1024)(128)(4,1)S(1)} %get-tuple-element.253, pred[3072]{0:T(1024)(128)(4,1)S(1)} %get-tuple-element.252, ...), kind=kLoop, calls=%fused_computation.61 | loop fusion | flops 294912 | bytes 230432 | tf_op jit(solution)/shard_map/div | solution.py:62
  69.0 2.3 %reduce-window.16 = f32[8,24,128]{2,1,0:T(8,128)S(1)} reduce-window(f32[8,24,128]{2,1,0:T(8,128)S(1)} %copy.55, f32[]{:T(128)} %constant.235.clone.1), window={size=1x1x128 pad=0_0x0_0x127_0}, to_apply=%region_5.6 | reduce-window | flops 3121152 | bytes 196612 | tf_op jit(solution)/shard_map/reduce-window.2
  72.4 8.3 %all-reduce.13 = f32[32]{0:T(128)S(1)} all-reduce(f32[32]{0:T(128)S(1)} %fusion.62), channel_id=3, replica_groups=mesh['person'=4,'var'=8] {'person'}, use_global_device_ids=true, to_apply=%add.13 | all-reduce | flops 32 | bytes 256
  81.0 3.7 %fusion.39 = bf16[8,3072]{0,1:T(8,128)(2,1)S(1)} fusion(f32[8,3072]{0,1:T(8,128)S(1)} %copy.58, f32[8,3072]{0,1:T(8,128)S(1)} %broadcast_add_fusion, f32[3072]{0:T(1024)S(1)} %convert_element_type.68, s32[8]{0:T(128)S(1)} %and_select_fusion, s32[3072]{0:T(1024)S(1)} %copy-done.1, pred[3072]{0:T(1024)(128)(4,1)S(1)} %get-tuple-element.256, ...), kind=kLoop, calls=%fused_computation.72 | loop fusion | flops 270336 | bytes 279584 | tf_op jit(solution)/shard_map/convert_element_type | solution.py:66
  84.7 9.2 %gather_fusion.1 = bf16[3072,8]{1,0:T(8,128)(2,1)S(1)} fusion(bf16[8,3072]{0,1:T(8,128)(2,1)S(1)} %fusion.39, s32[3072]{0:T(1024)S(1)} %fusion.60), kind=kCustom, calls=%fused_computation.1 | custom fusion | bytes 110592 | tf_op jit(solution)/shard_map/jit(_take)/gather | solution.py:73
  94.8 3.3 %all-to-all-start.1 = ((bf16[8,4,768]{2,0,1:T(8,128)(2,1)}), bf16[8,4,768]{2,0,1:T(8,128)(2,1)S(1)}, u32[]{:S(2)}, u32[]{:S(2)}) async-start(bf16[8,4,768]{2,0,1:T(8,128)(2,1)} %broadcast_select_fusion.4), calls=%async_computation.1 | async-start | bytes 98304 | tf_op jit(solution)/shard_map/all_to_all | solution.py:77
  98.2 5.6 %all-to-all-done.1 = bf16[8,4,768]{2,0,1:T(8,128)(2,1)S(1)} async-done(((bf16[8,4,768]{2,0,1:T(8,128)(2,1)}), bf16[8,4,768]{2,0,1:T(8,128)(2,1)S(1)}, u32[]{:S(2)}, u32[]{:S(2)}) %all-to-all-start.1) | async-done | bytes 49184 | tf_op jit(solution)/shard_map/all_to_all | solution.py:77
  104.2 8.5 %scatter_custom_fusion = bf16[8,3072]{0,1:T(8,128)(2,1)S(1)} fusion(s32[3072]{0:T(1024)S(1)} %bitcast.60, bf16[3072,8]{1,0:T(8,128)(2,1)S(1)} %copy.60, bf16[]{:T(256)} %constant.223.clone.1), kind=kCustom, calls=%fused_computation.75 | custom fusion | bytes 49154 | tf_op jit(solution)/shard_map/scatter | solution.py:81
  113.0 9.8 %all_gather.11 = bf16[64,3072]{1,0:T(8,128)(2,1)S(1)} all-gather(bf16[8,3072]{1,0:T(8,128)(2,1)S(1)} %copy.61), channel_id=1, replica_groups=mesh['person'=4,'var'=8] {'var'}, dimensions={0}, use_global_device_ids=true | all-gather | bytes 442368 | tf_op jit(solution)/shard_map/all_gather | solution.py:98
  123.5 1.2 fusion.90
  125.4 4.3 %fusion.15 = f32[64,2048]{1,0:T(8,128)S(1)} fusion(s32[512,2048]{1,0:T(8,128)} %param.18, bf16[64,512,1]{1,0,2:T(8,128)(2,1)S(1)} %copy.63), kind=kOutput, calls=%fused_computation.48 | convolution fusion | flops 141557760 | bytes 4784128 | tf_op jit(solution)/shard_map/dot_general | solution.py:105
  129.7 6.2 %convolution_add_fusion.4 = f32[64,2048]{1,0:T(8,128)S(1)} fusion(f32[64,2048]{1,0:T(8,128)S(1)} %fusion.15, s32[512,2048]{1,0:T(8,128)S(1)} %copy-done.7, bf16[64,512,1]{1,0,2:T(8,128)(2,1)S(1)} %copy.64), kind=kOutput, calls=%fused_computation.47 | convolution fusion | flops 150077440 | bytes 5308416 | tf_op jit(solution)/shard_map/dot_general | solution.py:105
  135.9 6.2 %convolution_add_fusion.3 = f32[64,2048]{1,0:T(8,128)S(1)} fusion(f32[64,2048]{1,0:T(8,128)S(1)} %convolution_add_fusion.4, s32[512,2048]{1,0:T(8,128)S(1)} %copy-done.7, bf16[64,512,1]{1,0,2:T(8,128)(2,1)S(1)} %copy.65), kind=kOutput, calls=%fused_computation.46 | convolution fusion | flops 150077440 | bytes 5308416 | tf_op jit(solution)/shard_map/dot_general | solution.py:105
  142.1 6.6 %convolution_add_fusion.2 = f32[64,2048]{1,0:T(8,128)S(1)} fusion(f32[64,2048]{1,0:T(8,128)S(1)} %convolution_add_fusion.3, s32[512,2048]{1,0:T(8,128)S(1)} %copy-done.7, bf16[64,512,1]{1,0,2:T(8,128)(2,1)S(1)} %copy.66), kind=kOutput, calls=%fused_computation.45 | convolution fusion | flops 150077440 | bytes 5308416 | tf_op jit(solution)/shard_map/dot_general | solution.py:105
  148.6 6.2 %convolution_add_fusion.1 = f32[64,2048]{1,0:T(8,128)S(1)} fusion(f32[64,2048]{1,0:T(8,128)S(1)} %convolution_add_fusion.2, s32[512,2048]{1,0:T(8,128)S(1)} %copy-done.7, bf16[64,512,1]{1,0,2:T(8,128)(2,1)S(1)} %copy.67), kind=kOutput, calls=%fused_computation.44 | convolution fusion | flops 150077440 | bytes 5308416 | tf_op jit(solution)/shard_map/dot_general | solution.py:105
  154.8 6.8 %convolution_add_fusion = f32[64,2048]{1,0:T(8,128)} fusion(f32[64,2048]{1,0:T(8,128)S(1)} %convolution_add_fusion.1, s32[512,2048]{1,0:T(8,128)S(1)} %copy-done.7, bf16[64,512,1]{1,0,2:T(8,128)(2,1)S(1)} %copy.68), kind=kOutput, calls=%fused_computation.43 | convolution fusion | flops 150077440 | bytes 5308416 | tf_op jit(solution)/shard_map/dot_general | solution.py:105
  161.6 36.0 %all-reduce.16.cloned.1.call-done = f32[64,2048]{1,0:T(8,128)} async-done(((f32[64,2048]{1,0:T(8,128)}), f32[64,2048]{1,0:T(8,128)}) %all-reduce.16.cloned.1.call-update) | async-done | bytes 524304 | tf_op jit(solution)/shard_map/psum | solution.py:109
  197.6 1.6 maximum_multiply_fusion
  (82 shorter events, 9.5 us)
Async XLA Ops:
  13.7 24.5 %copy-start.2 = (f32[8,3072]{1,0:T(8,128)S(1)}, f32[8,3072]{1,0:T(8,128)}, u32[]{:S(2)}) copy-start(f32[8,3072]{1,0:T(8,128)} %param.13) | copy-start | bytes 294916
  13.7 25.0 %copy-start.1 = (s32[3072]{0:T(1024)S(1)}, s32[3072]{0:T(1024)}, u32[]{:S(2)}) copy-start(s32[3072]{0:T(1024)} %param.15) | copy-start | bytes 36868
  31.8 63.0 %all-to-all-start = ((bf16[2,4,768]{2,0,1:T(2,128)(2,1)}), bf16[2,4,768]{2,0,1:T(2,128)(2,1)S(1)}, u32[]{:S(2)}, u32[]{:S(2)}) async-start(bf16[2,4,768]{2,0,1:T(2,128)(2,1)} %copy.50), calls=%async_computation | async-start | bytes 24576 | tf_op jit(solution)/shard_map/all_to_all | solution.py:78
  38.2 13.3 %copy-start.8 = (u32[32]{0:T(128)S(1)}, u32[32]{0:T(128)}, u32[]{:S(2)}) copy-start(u32[32]{0:T(128)} %constant.273) | copy-start | bytes 388
  40.1 25.3 %copy-start.4 = (s32[3072]{0:T(1024)S(1)}, s32[3072]{0:T(1024)}, u32[]{:S(2)}) copy-start(s32[3072]{0:T(1024)} %param.16) | copy-start | bytes 36868
  40.1 25.4 %copy-start.3 = (s32[3072]{0:T(1024)S(1)}, s32[3072]{0:T(1024)}, u32[]{:S(2)}) copy-start(s32[3072]{0:T(1024)} %param.14) | copy-start | bytes 36868
  94.8 9.0 %all-to-all-start.1 = ((bf16[8,4,768]{2,0,1:T(8,128)(2,1)}), bf16[8,4,768]{2,0,1:T(8,128)(2,1)S(1)}, u32[]{:S(2)}, u32[]{:S(2)}) async-start(bf16[8,4,768]{2,0,1:T(8,128)(2,1)} %broadcast_select_fusion.4), calls=%async_computation.1 | async-start | bytes 98304 | tf_op jit(solution)/shard_map/all_to_all | solution.py:77
  98.1 99.5 %all-reduce.16.cloned.1.call-start = ((), (), s32[]{:S(2)}) async-start(), calls=%async_computation.2 | async-start | bytes 1048576 | tf_op jit(solution)/shard_map/psum | solution.py:109
  125.4 4.3 %copy-start.7 = (s32[512,2048]{1,0:T(8,128)S(1)}, s32[512,2048]{1,0:T(8,128)}, u32[]{:S(2)}) copy-start(s32[512,2048]{1,0:T(8,128)} %param.18) | copy-start | bytes 12582916
  154.8 42.8 %copy-start = (s32[16,2048]{1,0:T(8,128)S(1)}, s32[16,2048]{1,0:T(8,128)}, u32[]{:S(2)}) copy-start(s32[16,2048]{1,0:T(8,128)} %param.21) | copy-start | bytes 393220
  154.8 42.8 %copy-start.5 = (f32[2048]{0:T(1024)S(1)}, f32[2048]{0:T(1024)}, u32[]{:S(2)}) copy-start(f32[2048]{0:T(1024)} %param.19) | copy-start | bytes 24580
  154.8 42.8 %copy-start.6 = (f32[16]{0:T(128)S(1)}, f32[16]{0:T(128)}, u32[]{:S(2)}) copy-start(f32[16]{0:T(128)} %param.20) | copy-start | bytes 196
Sparse Core Ops, SparseCore 0:
  161.8 35.8 all-reduce.15
where the time goes:
time: 207 us; the launch traced here: 206 us
  local copies, waits for them, and re-layouts  42.9 us (21%)
  waiting for transfers between devices  41.6 us (20%)
  matrix products  36.1 us (17%)
  other arithmetic  30.3 us (15%)
  blocking collectives  30.3 us (15%)
  between operations  15.1 us (7%)
  starting transfers between devices  9.64 us (5%)
    dot_general x6, matrix products, per_device(): jnp.dot(by_member[:, :, member], dosage, preferred_element_type=jnp.float32)  36.1 us
    psum x1, waiting for transfers between devices, per_device(): summed = lax.psum(scores, 'person')  36 us
    unnamed x2, blocking collectives  20.5 us
    gather x1, local copies, waits for them, and re-layouts, regroup(): place = jnp.take(file_index % width, order)  17.4 us
    another operation x7, other arithmetic  12.8 us
    all_gather x1, blocking collectives, per_device(): lax.all_gather(regroup(own_resid, time_order), 'var', axis=0, tiled=True)  9.77 us
    gather x2, local copies, waits for them, and re-layouts, regroup(): ordered = jnp.take(resid, order, axis=1)  9.41 us
    scatter x2, local copies, waits for them, and re-layouts, regroup(): return jnp.zeros_like(resid).at[:, slots].set(arrived)  8.78 us
  transfers between devices with their start and end apart: 3, of which 2 were waited for; matrix products, arithmetic and copies ran while one was open for 17% of the time, Pallas kernels for 0%

commit v1 on v0

v1 whole, which is shorter than its diff:
```python
import functools
import math

import jax
import jax.numpy as jnp
from jax import lax
from jax.experimental import pallas as pl
from jax.experimental.pallas import tpu as pltpu
from jax.sharding import PartitionSpec as P

FOLDS = 8
TIE_MAX = 4
MEMBERS = 6
LANES = 128
LOW = 256
PARTS = 4
CHUNKS = 4
MESH = pl.DeviceIdType.MESH


def each(count, body):
    if count <= 8:
        for step in range(count):
            body(step)
    else:
        lax.fori_loop(0, count, lambda step, none: (body(step), none)[1], 0)


def start_all(axis, size, me, source, buffer, send, recv):
    def one(step):
        peer = lax.rem(me + step + 1, size)
        pltpu.make_async_remote_copy(
            src_ref=source(peer),
            dst_ref=buffer.at[me],
            send_sem=send.at[step],
            recv_sem=recv.at[me],
            device_id={axis: peer},
            device_id_type=MESH,
        ).start()

    each(size - 1, one)


def wait_all(axis, size, me, source, buffer, send, recv, sent):
    def one(step):
        peer = lax.rem(me + step + 1, size)
        copy = pltpu.make_async_remote_copy(
            src_ref=source(peer),
            dst_ref=buffer.at[peer],
            send_sem=send.at[step],
            recv_sem=recv.at[peer],
            device_id={axis: peer},
            device_id_type=MESH,
        )
        if sent:
            copy.wait_send()
        else:
            copy.wait_recv()

    each(size - 1, one)


def cumulate(x, reverse):
    rows, width = x.shape
    count = width // LANES
    stacked = jnp.concatenate([x[:, c * LANES : (c + 1) * LANES] for c in range(count)], axis=0)
    high = stacked.astype(jnp.bfloat16)
    rest = stacked - high.astype(jnp.float32)
    middle = rest.astype(jnp.bfloat16)
    low = (rest - middle.astype(jnp.float32)).astype(jnp.bfloat16)
    split = jnp.concatenate([high, middle, low], axis=1)
    row = lax.broadcasted_iota(jnp.int32, (3 * LANES, 2 * LANES), 0) & (LANES - 1)
    col = lax.broadcasted_iota(jnp.int32, (3 * LANES, 2 * LANES), 1)
    inside = (row >= col) if reverse else (row <= col)
    ones = jnp.where(inside | (col >= LANES), 1.0, 0.0).astype(jnp.bfloat16)
    sums = jnp.dot(split, ones, preferred_element_type=jnp.float32)
    carry = jnp.zeros((rows, LANES), jnp.float32)
    pieces = [None] * count
    for c in reversed(range(count)) if reverse else range(count):
        pieces[c] = sums[c * rows : (c + 1) * rows, :LANES] + carry
        carry = carry + sums[c * rows : (c + 1) * rows, LANES:]
    return jnp.concatenate(pieces, axis=1), carry


def over_group(values, tie, forward):
    width = values.shape[1]
    result = values
    for offset in range(1, TIE_MAX):
        by = offset if forward else width - offset
        same = pltpu.roll(tie, by, 1) == tie
        result = jnp.maximum(result, jnp.where(same, pltpu.roll(values, by, 1), 0.0))
    return result


def kernel(
    n_person,
    n_var,
    pred_ref,
    event_ref,
    fold_ref,
    tie_ref,
    order_ref,
    geno_hbm,
    scale_ref,
    penalty_ref,
    strong_ref,
    gradient_ref,
    violation_ref,
    geno,
    dosage,
    onehot,
    risk_totals,
    hazard_totals,
    outgoing,
    arrived,
    file_order,
    lhs,
    partial,
    summands,
    geno_sem,
    sems_send,
    sems_recv,
    var_send,
    var_recv,
    sum_send,
    sum_recv,
):
    f32, bf16 = jnp.float32, jnp.bfloat16
    me = lax.axis_index("person")
    here = lax.axis_index("var")
    kl, width = pred_ref.shape
    words, variants = geno.shape
    high = MEMBERS * words // LOW
    part = words // PARTS
    chunk = variants // CHUNKS
    share = gradient_ref.shape[0]

    def geno_copy(q):
        rows = pl.ds(q * part, part)
        return pltpu.make_async_copy(geno_hbm.at[rows], geno.at[rows], geno_sem.at[q])

    for q in range(PARTS):
        geno_copy(q).start()

    barrier = pltpu.get_barrier_semaphore()

    def greet(axis, size, mine):
        def one(step):
            peer = lax.rem(mine + step + 1, size)
            pl.semaphore_signal(barrier, inc=1, device_id={axis: peer}, device_id_type=MESH)

        each(size - 1, one)

    greet("person", n_person, me)
    greet("var", n_var, here)

    def decode(q):
        geno_copy(q).wait()
        piece = min(512, variants)

        def block(step, none):
            at = pl.multiple_of(q * part + step * 16, 16)
            for c in range(variants // piece):
                cols = slice(c * piece, (c + 1) * piece)
                left = geno[pl.ds(at, 16), cols].astype(f32)
                for member in range(MEMBERS):
                    if member < MEMBERS - 1:
                        above = jnp.floor(left * (1.0 / 3.0) + (1.0 / 6.0))
                        digit = left - 3.0 * above
                        left = above
                    else:
                        digit = left
                    to = pl.multiple_of(member * words + at, 16)
                    dosage[pl.ds(to, 16), cols] = digit.astype(bf16)
            return none

        lax.fori_loop(0, part // 16, block, 0)

    column = here * kl + lax.broadcasted_iota(jnp.int32, (kl, width), 0)
    weight = jnp.where(fold_ref[...] != lax.rem(column, FOLDS), 1.0, 0.0)
    events = event_ref[...].astype(f32)
    tie = jnp.broadcast_to(tie_ref[...], (kl, width))
    risk = jnp.exp(pred_ref[...])
    suffix, total = cumulate(weight * risk, True)
    risk_totals[me] = total
    pl.semaphore_wait(barrier, n_person + n_var - 2)

    def risk_source(peer):
        return risk_totals.at[me]

    def hazard_source(peer):
        return hazard_totals.at[me]

    start_all("person", n_person, me, risk_source, risk_totals, sems_send.at[0], sems_recv.at[0])

    base = over_group(suffix, tie, True) + 1.0 - weight
    numerator = weight * events
    word = jnp.floor((order_ref[...].astype(f32) + 0.5) * (1.0 / MEMBERS))
    member = order_ref[...] - MEMBERS * word.astype(jnp.int32)
    block = jnp.floor((word + 0.5) * (1.0 / words)).astype(jnp.int32)
    inner = word.astype(jnp.int32) - words * block
    upper = jnp.floor((inner.astype(f32) + 0.5) * (1.0 / LOW)).astype(jnp.int32)
    lower = inner - LOW * upper
    key = jnp.broadcast_to(block * high + member * (words // LOW) + upper, (kl, width))
    lane = lax.broadcasted_iota(jnp.int32, (LOW, LANES), 0)
    for c in range(width // LANES):
        cols = slice(c * LANES, (c + 1) * LANES)
        onehot[:, cols] = jnp.where(lane == lower[:, cols], 1.0, 0.0).astype(bf16)
    decode(0)

    wait_all("person", n_person, me, risk_source, risk_totals, sems_send.at[0], sems_recv.at[0], False)

    def carried(buffer, later):
        total = jnp.zeros((kl, LANES), f32)
        for k in range(n_person):
            at = n_person - 1 - k if later else k
            wanted = at > me if later else at < me
            total = total + jnp.where(wanted, buffer[at], 0.0)
        return jnp.concatenate([total] * (width // LANES), axis=1)

    hazard = numerator / (base + carried(risk_totals, True))
    prefix, total = cumulate(hazard, False)
    hazard_totals[me] = total
    start_all("person", n_person, me, hazard_source, hazard_totals, sems_send.at[1], sems_recv.at[1])
    last = over_group(prefix, tie, False)
    decode(1)
    wait_all("person", n_person, me, hazard_source, hazard_totals, sems_send.at[1], sems_recv.at[1], False)
    resid = weight * (events - risk * (last + carried(hazard_totals, False)))

    def for_block(to):
        first = to * high
        rows = [jnp.where(key == first + h, resid, 0.0).astype(f32) for h in range(high)]
        picked = jnp.concatenate(rows, axis=0).astype(bf16)
        return lax.dot_general(
            picked, onehot[...], (((1,), (1,)), ((), ())), preferred_element_type=f32
        ).astype(bf16)

    def out_source(peer):
        return outgoing.at[peer]

    def regroup(step):
        peer = lax.rem(me + step + 1, n_person)
        outgoing[peer] = for_block(peer)
        pltpu.make_async_remote_copy(
            src_ref=outgoing.at[peer],
            dst_ref=arrived.at[me],
            send_sem=sems_send.at[2, step],
            recv_sem=sems_recv.at[2, me],
            device_id={"person": peer},
            device_id_type=MESH,
        ).start()

    each(n_person - 1, regroup)
    arrived[me] = for_block(me)
    decode(2)
    wait_all("person", n_person, me, out_source, arrived, sems_send.at[2], sems_recv.at[2], False)
    own = arrived[0].astype(f32)
    for k in range(1, n_person):
        own = own + arrived[k].astype(f32)
    file_order[here] = own.astype(bf16)

    def file_source(peer):
        return file_order.at[here]

    start_all("var", n_var, here, file_source, file_order, var_send, var_recv)
    decode(3)
    wait_all("var", n_var, here, file_source, file_order, var_send, var_recv, False)
    gathered = [file_order[v].astype(f32) for v in range(n_var)]
    for h in range(high):
        rows = [x[h * kl : (h + 1) * kl] for x in gathered]
        lhs[:, h * LOW : (h + 1) * LOW] = jnp.concatenate(rows, axis=0).astype(bf16)

    for c in range(CHUNKS):
        def tile(step, none):
            at = pl.multiple_of(step * LOW, LOW)
            cols = pl.ds(pl.multiple_of(c * chunk + step * LOW, LOW), LOW)
            product = jnp.dot(lhs[...], dosage[:, cols], preferred_element_type=f32)
            for k in range(n_person):
                partial[c, k, :, pl.ds(at, LOW)] = product[k * share : (k + 1) * share]
            return none

        lax.fori_loop(0, chunk // LOW, tile, 0)
        summands[c, me] = partial[c, me]

        def sum_source(peer):
            return partial.at[c, peer]

        start_all("person", n_person, me, sum_source, summands.at[c], sum_send.at[c], sum_recv.at[c])

    row = lax.broadcasted_iota(jnp.int32, (share, share), 0)
    col = lax.broadcasted_iota(jnp.int32, (share, share), 1)
    penalty = jnp.sum(jnp.where(row == col, penalty_ref[...], 0.0), axis=1, keepdims=True)
    factor = 1.0 / math.sqrt(width * n_person)
    for c in range(CHUNKS):
        def sum_source(peer):
            return partial.at[c, peer]

        wait_all("person", n_person, me, sum_source, summands.at[c], sum_send.at[c], sum_recv.at[c], False)
        cols = slice(c * chunk, (c + 1) * chunk)
        mine = summands[c, 0]
        for k in range(1, n_person):
            mine = mine + summands[c, k]
        gradient = mine * (scale_ref[:, cols] * factor)
        gradient_ref[:, cols] = gradient
        violation_ref[:, cols] = (1 - strong_ref[:, cols]).astype(f32) * jnp.maximum(
            jnp.abs(gradient) - penalty, 0.0
        )

    wait_all("person", n_person, me, risk_source, risk_totals, sems_send.at[0], sems_recv.at[0], True)
    wait_all("person", n_person, me, hazard_source, hazard_totals, sems_send.at[1], sems_recv.at[1], True)
    wait_all("person", n_person, me, out_source, arrived, sems_send.at[2], sems_recv.at[2], True)
    wait_all("var", n_var, here, file_source, file_order, var_send, var_recv, True)
    for c in range(CHUNKS):
        def sum_source(peer):
            return partial.at[c, peer]

        wait_all("person", n_person, me, sum_source, summands.at[c], sum_send.at[c], sum_recv.at[c], True)


def per_device(
    n_person,
    n_var,
    linear_pred,
    event_flag,
    fold_id,
    tie_group,
    time_order,
    genotypes,
    variant_scale,
    penalty,
    strong_set,
):
    kl, width = linear_pred.shape
    words, variants = genotypes.shape
    share = strong_set.shape[0]
    columns = kl * n_var
    rows = MEMBERS * words // LOW * kl
    f32, bf16, dma = jnp.float32, jnp.bfloat16, pltpu.SemaphoreType.DMA
    vmem = pl.BlockSpec(memory_space=pltpu.VMEM)
    out = jax.ShapeDtypeStruct((share, variants), f32)
    return pl.pallas_call(
        functools.partial(kernel, n_person, n_var),
        out_shape=(out, out),
        in_specs=[vmem] * 5 + [pl.BlockSpec(memory_space=pl.ANY)] + [vmem] * 3,
        out_specs=(vmem, vmem),
        scratch_shapes=[
            pltpu.VMEM((words, variants), jnp.int32),
            pltpu.VMEM((MEMBERS * words, variants), bf16),
            pltpu.VMEM((LOW, width), bf16),
            pltpu.VMEM((n_person, kl, LANES), f32),
            pltpu.VMEM((n_person, kl, LANES), f32),
            pltpu.VMEM((n_person, rows, LOW), bf16),
            pltpu.VMEM((n_person, rows, LOW), bf16),
            pltpu.VMEM((n_var, rows, LOW), bf16),
            pltpu.VMEM((columns, MEMBERS * words), bf16),
            pltpu.VMEM((CHUNKS, n_person, share, variants // CHUNKS), f32),
            pltpu.VMEM((CHUNKS, n_person, share, variants // CHUNKS), f32),
            dma((PARTS,)),
            dma((3, n_person)),
            dma((3, n_person)),
            dma((n_var,)),
            dma((n_var,)),
            dma((CHUNKS, n_person)),
            dma((CHUNKS, n_person)),
        ],
        compiler_params=pltpu.CompilerParams(
            collective_id=0, has_side_effects=True, vmem_limit_bytes=56 * 2**20
        ),
    )(
        linear_pred,
        event_flag[None],
        fold_id[None],
        tie_group[None],
        time_order[None],
        genotypes,
        variant_scale[None],
        penalty[None],
        strong_set,
    )


def solution(mesh):
    placed = (
        P("var", "person"),
        P("person"),
        P("person"),
        P("person"),
        P("person"),
        P("person", "var"),
        P("var"),
        P("person"),
        P("person", "var"),
    )
    return jax.shard_map(
        functools.partial(per_device, mesh.shape["person"], mesh.shape["var"]),
        mesh=mesh,
        in_specs=placed,
        out_specs=(P("person", "var"), P("person", "var")),
        check_vma=False,
    )
```

time: 207 us -> 43.6 us (0.21)
  waiting for transfers between devices: 41.6 us -> 0 us
  local copies, waits for them, and re-layouts: 42.9 us -> 3.14 us
  Pallas kernels: 0 us -> 39.7 us
  matrix products: 36.1 us -> 0 us
  other arithmetic: 30.3 us -> 0 us
  blocking collectives: 30.3 us -> 0 us
  between operations: 15.1 us -> 0.64 us
  starting transfers between devices: 9.64 us -> 0 us
    pallas_call x0 -> x1, Pallas kernels: none -> 39.7 us  [per_device(): pl.pallas_call(functools.partial(kernel, n_person, n_var), out_shape=(out...]
    dot_general x6 -> x0, matrix products: 36.1 us -> none  [per_device(): jnp.dot(by_member[:, :, member], dosage, preferred_element_type=jnp.float32)]
    psum x1 -> x0, waiting for transfers between devices: 36 us -> none  [per_device(): summed = lax.psum(scores, 'person')]
    gather x3 -> x0, local copies, waits for them, and re-layouts: 26.8 us -> none  [the longest x1 17.4 us: regroup(): place = jnp.take(file_index % width, order)]
    unnamed x2 -> x0, blocking collectives: 20.5 us -> none
    another operation x9 -> x0, other arithmetic: 12.9 us -> none
    all_gather x1 -> x0, blocking collectives: 9.77 us -> none  [per_device(): lax.all_gather(regroup(own_resid, time_order), 'var', axis=0, tiled=True)]
    all_to_all x2 -> x0, starting transfers between devices: 9.6 us -> none  [the longest x1 6.32 us: regroup(): lax.all_to_all(digits, 'person', split_axis=1, concat_axis=1, tiled=True)]
  transfers between devices with their start and end apart: 3 -> 0, of which waited for: 2 -> 0; matrix products, arithmetic and copies ran while one was open for 17% -> 0% of each run, Pallas kernels for 0% -> 0%
where the time goes in v1:
time: 43.6 us; the launch traced here: 43.4 us
  Pallas kernels  39.7 us (91%)
  local copies, waits for them, and re-layouts  3.14 us (7%)
  between operations  0.64 us (1%)
    pallas_call x1, Pallas kernels, per_device(): pl.pallas_call(functools.partial(kernel, n_person, n_var), out_shape=(out...  39.7 us
    unnamed x2, local copies, waits for them, and re-layouts  3.14 us

profile of v1, /device:TPU:0, one launch (start us, length us, event | category | flops | bytes accessed | tf_op | source)
XLA Modules:
  0.0 43.4 jit_solution(5086614184203468969)
XLA Ops:
  0.6 39.7 %shard_map.104 = (f32[16,2048]{1,0:T(8,128)}, f32[16,2048]{1,0:T(8,128)}) custom-call(f32[8,3072]{1,0:T(8,128)} %pred_ref.1, s32[1,3072]{1,0:T(1,128)} %bitcast.6, s32[1,3072]{1,0:T(1,128)} %bitcast.7, s32[1,3072]{1,0:T(1,128)} %bitcast.8, s32[1,3072]{1,0:T(1,128)} %bitcast.9, s32[512,2048]{1,0:T(8,128)} %geno_hbm.1, f32[1,2048]{1,0:T(1,128)} %bitcast.10, ...), custom_call_target="tpu_custom_call" | custom-call | tf_op jit(solution)/shard_map/pallas_call | solution.py:341
  40.3 1.6 %copy.13 = f32[16,2048]{1,0:T(8,128)} copy(f32[16,2048]{1,0:T(8,128)} %get-tuple-element.4) | data formatting | bytes 262144
  41.9 1.6 %copy.14 = f32[16,2048]{1,0:T(8,128)} copy(f32[16,2048]{1,0:T(8,128)} %get-tuple-element.5) | data formatting | bytes 262144

commit v2 on v1

--- a/solution.py
+++ b/solution.py
@@ -101,11 +101,7 @@
     tie_ref,
     order_ref,
     geno_hbm,
-    scale_ref,
-    penalty_ref,
-    strong_ref,
-    gradient_ref,
-    violation_ref,
+    summed_ref,
     geno,
     dosage,
     onehot,
@@ -115,6 +111,7 @@
     arrived,
     file_order,
     lhs,
+    own_part,
     partial,
     summands,
     geno_sem,
@@ -133,7 +130,7 @@
     high = MEMBERS * words // LOW
     part = words // PARTS
     chunk = variants // CHUNKS
-    share = gradient_ref.shape[0]
+    share = summed_ref.shape[0]
 
     def geno_copy(q):
         rows = pl.ds(q * part, part)
@@ -276,35 +273,28 @@
             cols = pl.ds(pl.multiple_of(c * chunk + step * LOW, LOW), LOW)
             product = jnp.dot(lhs[...], dosage[:, cols], preferred_element_type=f32)
             for k in range(n_person):
-                partial[c, k, :, pl.ds(at, LOW)] = product[k * share : (k + 1) * share]
+                rows = product[k * share : (k + 1) * share]
+                partial[c, k, :, pl.ds(at, LOW)] = rows.astype(bf16)
+                own_part[k, :, cols] = rows
             return none
 
         lax.fori_loop(0, chunk // LOW, tile, 0)
-        summands[c, me] = partial[c, me]
 
         def sum_source(peer):
             return partial.at[c, peer]
 
         start_all("person", n_person, me, sum_source, summands.at[c], sum_send.at[c], sum_recv.at[c])
 
-    row = lax.broadcasted_iota(jnp.int32, (share, share), 0)
-    col = lax.broadcasted_iota(jnp.int32, (share, share), 1)
-    penalty = jnp.sum(jnp.where(row == col, penalty_ref[...], 0.0), axis=1, keepdims=True)
-    factor = 1.0 / math.sqrt(width * n_person)
     for c in range(CHUNKS):
         def sum_source(peer):
             return partial.at[c, peer]
 
         wait_all("person", n_person, me, sum_source, summands.at[c], sum_send.at[c], sum_recv.at[c], False)
         cols = slice(c * chunk, (c + 1) * chunk)
-        mine = summands[c, 0]
-        for k in range(1, n_person):
-            mine = mine + summands[c, k]
-        gradient = mine * (scale_ref[:, cols] * factor)
-        gradient_ref[:, cols] = gradient
-        violation_ref[:, cols] = (1 - strong_ref[:, cols]).astype(f32) * jnp.maximum(
-            jnp.abs(gradient) - penalty, 0.0
-        )
+        mine = own_part[me, :, cols]
+        for k in range(n_person):
+            mine = mine + jnp.where(k == me, 0.0, summands[c, k].astype(f32))
+        summed_ref[:, cols] = mine
 
     wait_all("person", n_person, me, risk_source, risk_totals, sems_send.at[0], sems_recv.at[0], True)
     wait_all("person", n_person, me, hazard_source, hazard_totals, sems_send.at[1], sems_recv.at[1], True)
@@ -337,12 +327,11 @@
     rows = MEMBERS * words // LOW * kl
     f32, bf16, dma = jnp.float32, jnp.bfloat16, pltpu.SemaphoreType.DMA
     vmem = pl.BlockSpec(memory_space=pltpu.VMEM)
-    out = jax.ShapeDtypeStruct((share, variants), f32)
-    return pl.pallas_call(
+    summed = pl.pallas_call(
         functools.partial(kernel, n_person, n_var),
-        out_shape=(out, out),
-        in_specs=[vmem] * 5 + [pl.BlockSpec(memory_space=pl.ANY)] + [vmem] * 3,
-        out_specs=(vmem, vmem),
+        out_shape=jax.ShapeDtypeStruct((share, variants), f32),
+        in_specs=[vmem] * 5 + [pl.BlockSpec(memory_space=pl.ANY)],
+        out_specs=vmem,
         scratch_shapes=[
             pltpu.VMEM((words, variants), jnp.int32),
             pltpu.VMEM((MEMBERS * words, variants), bf16),
@@ -353,8 +342,9 @@
             pltpu.VMEM((n_person, rows, LOW), bf16),
             pltpu.VMEM((n_var, rows, LOW), bf16),
             pltpu.VMEM((columns, MEMBERS * words), bf16),
-            pltpu.VMEM((CHUNKS, n_person, share, variants // CHUNKS), f32),
-            pltpu.VMEM((CHUNKS, n_person, share, variants // CHUNKS), f32),
+            pltpu.VMEM((n_person, share, variants), f32),
+            pltpu.VMEM((CHUNKS, n_person, share, variants // CHUNKS), bf16),
+            pltpu.VMEM((CHUNKS, n_person, share, variants // CHUNKS), bf16),
             dma((PARTS,)),
             dma((3, n_person)),
             dma((3, n_person)),
@@ -373,10 +363,12 @@
         tie_group[None],
         time_order[None],
         genotypes,
-        variant_scale[None],
-        penalty[None],
-        strong_set,
     )
+    gradient = summed * (variant_scale[None, :] / math.sqrt(width * n_person))
+    violation = (1 - strong_set).astype(f32) * jnp.maximum(
+        jnp.abs(gradient) - penalty[:, None], 0.0
+    )
+    return gradient, violation
 
 
 def solution(mesh):

time: 43.6 us -> 37.5 us (0.86)
  Pallas kernels: 39.7 us -> 34.2 us
  local copies, waits for them, and re-layouts: 3.14 us -> 0.01 us
  other arithmetic: 0 us -> 2.38 us
    pallas_call x1, Pallas kernels: 39.7 us -> 34.2 us  [per_device(): pl.pallas_call(functools.partial(kernel, n_person, n_var), out_shape=jax....]
    unnamed x2 -> x4, local copies, waits for them, and re-layouts: 3.14 us -> 0.01 us
    mul x0 -> x1, other arithmetic: none -> 1.64 us  [per_device(): (1 - strong_set).astype(f32)]
    div x0 -> x1, other arithmetic: none -> 0.73 us  [per_device(): gradient = summed * (variant_scale[None, :] / math.sqrt(width * n_person))]
where the time goes in v2:
time: 37.5 us; the launch traced here: 37.2 us
  Pallas kernels  34.2 us (91%)
  other arithmetic  2.38 us (6%)
  between operations  0.67 us (2%)
    pallas_call x1, Pallas kernels, per_device(): pl.pallas_call(functools.partial(kernel, n_person, n_var), out_shape=jax....  34.2 us
    mul x1, other arithmetic, per_device(): (1 - strong_set).astype(f32)  1.64 us

profile of v2, /device:TPU:0, one launch (start us, length us, event | category | flops | bytes accessed | tf_op | source)
XLA Modules:
  0.0 37.2 jit_solution(4179163833128071740)
XLA Ops:
  0.6 0.0 copy-start
  0.6 0.0 copy-start.1
  0.7 0.7 %broadcast_multiply_fusion.1 = f32[2048]{0:T(1024)S(1)} fusion(f32[2048]{0:T(1024)} %param.15), kind=kLoop, calls=%fused_computation.2 | loop fusion | flops 2048 | bytes 16384 | tf_op jit(solution)/shard_map/div | solution.py:367
  1.4 34.2 %shard_map.104 = f32[16,2048]{1,0:T(8,128)} custom-call(f32[8,3072]{1,0:T(8,128)} %pred_ref.1, s32[1,3072]{1,0:T(1,128)} %bitcast.4, s32[1,3072]{1,0:T(1,128)} %bitcast.5, s32[1,3072]{1,0:T(1,128)} %bitcast.6, s32[1,3072]{1,0:T(1,128)} %bitcast.7, s32[512,2048]{1,0:T(8,128)} %geno_hbm.1), custom_call_target="tpu_custom_call" | custom-call | tf_op jit(solution)/shard_map/pallas_call | solution.py:330
  35.6 0.0 copy-done
  35.6 0.0 copy-done.1
  35.6 1.6 %maximum_multiply_fusion = (f32[16,2048]{1,0:T(8,128)}, f32[16,2048]{1,0:T(8,128)}) fusion(s32[16,2048]{1,0:T(8,128)S(1)} %copy-done, f32[16]{0:T(128)S(1)} %copy-done.1, f32[16,2048]{1,0:T(8,128)} %shard_map.104, f32[2048]{0:T(1024)S(1)} %broadcast_multiply_fusion.1), kind=kLoop, calls=%fused_computation | loop fusion | flops 229376 | bytes 532544 | tf_op jit(solution)/shard_map/mul | solution.py:368
Async XLA Ops:
  0.6 34.9 %copy-start = (s32[16,2048]{1,0:T(8,128)S(1)}, s32[16,2048]{1,0:T(8,128)}, u32[]{:S(2)}) copy-start(s32[16,2048]{1,0:T(8,128)} %param.17) | copy-start | bytes 393220
  0.6 34.9 %copy-start.1 = (f32[16]{0:T(128)S(1)}, f32[16]{0:T(128)}, u32[]{:S(2)}) copy-start(f32[16]{0:T(128)} %param.16) | copy-start | bytes 196

commit v3 on v2

--- a/solution.py
+++ b/solution.py
@@ -114,6 +114,10 @@
     own_part,
     partial,
     summands,
+    levels,
+    levels_in,
+    means,
+    counts,
     geno_sem,
     sems_send,
     sems_recv,
@@ -121,6 +125,8 @@
     var_recv,
     sum_send,
     sum_recv,
+    side_send,
+    side_recv,
 ):
     f32, bf16 = jnp.float32, jnp.bfloat16
     me = lax.axis_index("person")
@@ -160,6 +166,7 @@
             for c in range(variants // piece):
                 cols = slice(c * piece, (c + 1) * piece)
                 left = geno[pl.ds(at, 16), cols].astype(f32)
+                count = counts[:, cols]
                 for member in range(MEMBERS):
                     if member < MEMBERS - 1:
                         above = jnp.floor(left * (1.0 / 3.0) + (1.0 / 6.0))
@@ -167,8 +174,10 @@
                         left = above
                     else:
                         digit = left
+                    count = count + digit
                     to = pl.multiple_of(member * words + at, 16)
                     dosage[pl.ds(to, 16), cols] = digit.astype(bf16)
+                counts[:, cols] = count
             return none
 
         lax.fori_loop(0, part // 16, block, 0)
@@ -203,6 +212,7 @@
     for c in range(width // LANES):
         cols = slice(c * LANES, (c + 1) * LANES)
         onehot[:, cols] = jnp.where(lane == lower[:, cols], 1.0, 0.0).astype(bf16)
+    counts[...] = jnp.zeros_like(counts)
     decode(0)
 
     wait_all("person", n_person, me, risk_source, risk_totals, sems_send.at[0], sems_recv.at[0], False)
@@ -261,20 +271,39 @@
 
     start_all("var", n_var, here, file_source, file_order, var_send, var_recv)
     decode(3)
+    means[me] = jnp.sum(counts[...], axis=0, keepdims=True) * (1.0 / (MEMBERS * words))
+
+    def mean_source(peer):
+        return means.at[me]
+
+    start_all("person", n_person, me, mean_source, means, side_send.at[1], side_recv.at[1])
     wait_all("var", n_var, here, file_source, file_order, var_send, var_recv, False)
     gathered = [file_order[v].astype(f32) for v in range(n_var)]
+    columns = n_var * kl
+    level = jnp.zeros((columns, LOW), f32)
     for h in range(high):
-        rows = [x[h * kl : (h + 1) * kl] for x in gathered]
-        lhs[:, h * LOW : (h + 1) * LOW] = jnp.concatenate(rows, axis=0).astype(bf16)
+        rows = jnp.concatenate([x[h * kl : (h + 1) * kl] for x in gathered], axis=0)
+        lhs[:, h * LOW : (h + 1) * LOW] = rows.astype(bf16)
+        level = level + rows
+    level = jnp.sum(level, axis=1, keepdims=True)
+    for k in range(n_person):
+        levels[k] = jnp.broadcast_to(level[k * share : (k + 1) * share], (share, LANES))
+
+    def level_source(peer):
+        return levels.at[peer]
+
+    start_all("person", n_person, me, level_source, levels_in, side_send.at[0], side_recv.at[0])
 
     for c in range(CHUNKS):
         def tile(step, none):
             at = pl.multiple_of(step * LOW, LOW)
             cols = pl.ds(pl.multiple_of(c * chunk + step * LOW, LOW), LOW)
             product = jnp.dot(lhs[...], dosage[:, cols], preferred_element_type=f32)
+            mean = means[me, :, cols]
             for k in range(n_person):
                 rows = product[k * share : (k + 1) * share]
-                partial[c, k, :, pl.ds(at, LOW)] = rows.astype(bf16)
+                centred = rows - level[k * share : (k + 1) * share] * mean
+                partial[c, k, :, pl.ds(at, LOW)] = centred.astype(bf16)
                 own_part[k, :, cols] = rows
             return none
 
@@ -285,6 +314,8 @@
 
         start_all("person", n_person, me, sum_source, summands.at[c], sum_send.at[c], sum_recv.at[c])
 
+    wait_all("person", n_person, me, level_source, levels_in, side_send.at[0], side_recv.at[0], False)
+    wait_all("person", n_person, me, mean_source, means, side_send.at[1], side_recv.at[1], False)
     for c in range(CHUNKS):
         def sum_source(peer):
             return partial.at[c, peer]
@@ -293,13 +324,16 @@
         cols = slice(c * chunk, (c + 1) * chunk)
         mine = own_part[me, :, cols]
         for k in range(n_person):
-            mine = mine + jnp.where(k == me, 0.0, summands[c, k].astype(f32))
+            other = summands[c, k].astype(f32) + levels_in[k][:, :1] * means[k, :, cols]
+            mine = mine + jnp.where(k == me, 0.0, other)
         summed_ref[:, cols] = mine
 
     wait_all("person", n_person, me, risk_source, risk_totals, sems_send.at[0], sems_recv.at[0], True)
     wait_all("person", n_person, me, hazard_source, hazard_totals, sems_send.at[1], sems_recv.at[1], True)
     wait_all("person", n_person, me, out_source, arrived, sems_send.at[2], sems_recv.at[2], True)
     wait_all("var", n_var, here, file_source, file_order, var_send, var_recv, True)
+    wait_all("person", n_person, me, level_source, levels_in, side_send.at[0], side_recv.at[0], True)
+    wait_all("person", n_person, me, mean_source, means, side_send.at[1], side_recv.at[1], True)
     for c in range(CHUNKS):
         def sum_source(peer):
             return partial.at[c, peer]
@@ -345,6 +379,10 @@
             pltpu.VMEM((n_person, share, variants), f32),
             pltpu.VMEM((CHUNKS, n_person, share, variants // CHUNKS), bf16),
             pltpu.VMEM((CHUNKS, n_person, share, variants // CHUNKS), bf16),
+            pltpu.VMEM((n_person, share, LANES), f32),
+            pltpu.VMEM((n_person, share, LANES), f32),
+            pltpu.VMEM((n_person, 1, variants), f32),
+            pltpu.VMEM((16, variants), f32),
             dma((PARTS,)),
             dma((3, n_person)),
             dma((3, n_person)),
@@ -352,6 +390,8 @@
             dma((n_var,)),
             dma((CHUNKS, n_person)),
             dma((CHUNKS, n_person)),
+            dma((2, n_person)),
+            dma((2, n_person)),
         ],
         compiler_params=pltpu.CompilerParams(
             collective_id=0, has_side_effects=True, vmem_limit_bytes=56 * 2**20
@@ -364,7 +404,7 @@
         time_order[None],
         genotypes,
     )
-    gradient = summed * (variant_scale[None, :] / math.sqrt(width * n_person))
+    gradient = summed * variant_scale[None, :] * (1.0 / math.sqrt(width * n_person))
     violation = (1 - strong_set).astype(f32) * jnp.maximum(
         jnp.abs(gradient) - penalty[:, None], 0.0
     )

time: 37.5 us -> 37.4 us (level)
  other arithmetic: 2.38 us -> 1.64 us
  Pallas kernels: 34.2 us -> 34.9 us
    pallas_call x1, Pallas kernels: 34.2 us -> 34.9 us  [per_device(): pl.pallas_call(functools.partial(kernel, n_person, n_var), out_shape=jax....]
    div x1 -> x0, other arithmetic: 0.73 us -> none  [per_device(): gradient = summed * (variant_scale[None, :] / math.sqrt(width * n_person))]
where the time goes in v3:
time: 37.4 us; the launch traced here: 37.3 us
  Pallas kernels  34.9 us (93%)
  other arithmetic  1.64 us (4%)
  between operations  0.69 us (2%)
    pallas_call x1, Pallas kernels, per_device(): pl.pallas_call(functools.partial(kernel, n_person, n_var), out_shape=jax....  34.9 us
    mul x1, other arithmetic, per_device(): (1 - strong_set).astype(f32)  1.64 us

profile of v3, /device:TPU:0, one launch (start us, length us, event | category | flops | bytes accessed | tf_op | source)
XLA Modules:
  0.0 37.3 jit_solution(8511158963199696294)
XLA Ops:
  0.6 0.0 copy-start
  0.6 0.0 copy-start.2
  0.7 0.0 copy-start.1
  0.7 34.9 %shard_map.104 = f32[16,2048]{1,0:T(8,128)} custom-call(f32[8,3072]{1,0:T(8,128)} %pred_ref.1, s32[1,3072]{1,0:T(1,128)} %bitcast.4, s32[1,3072]{1,0:T(1,128)} %bitcast.5, s32[1,3072]{1,0:T(1,128)} %bitcast.6, s32[1,3072]{1,0:T(1,128)} %bitcast.7, s32[512,2048]{1,0:T(8,128)} %geno_hbm.1), custom_call_target="tpu_custom_call" | custom-call | tf_op jit(solution)/shard_map/pallas_call | solution.py:364
  35.6 0.0 copy-done
  35.6 0.0 copy-done.2
  35.6 0.0 copy-done.1
  35.6 1.6 %maximum_multiply_fusion = (f32[16,2048]{1,0:T(8,128)}, f32[16,2048]{1,0:T(8,128)}) fusion(s32[16,2048]{1,0:T(8,128)S(1)} %copy-done, f32[16]{0:T(128)S(1)} %copy-done.2, f32[16,2048]{1,0:T(8,128)} %shard_map.104, f32[2048]{0:T(1024)S(1)} %copy-done.1), kind=kLoop, calls=%fused_computation | loop fusion | flops 262144 | bytes 532544 | tf_op jit(solution)/shard_map/mul | solution.py:408
Async XLA Ops:
  0.6 35.0 %copy-start = (s32[16,2048]{1,0:T(8,128)S(1)}, s32[16,2048]{1,0:T(8,128)}, u32[]{:S(2)}) copy-start(s32[16,2048]{1,0:T(8,128)} %param.17) | copy-start | bytes 393220
  0.6 35.0 %copy-start.2 = (f32[16]{0:T(128)S(1)}, f32[16]{0:T(128)}, u32[]{:S(2)}) copy-start(f32[16]{0:T(128)} %param.16) | copy-start | bytes 196
  0.7 35.0 %copy-start.1 = (f32[2048]{0:T(1024)S(1)}, f32[2048]{0:T(1024)}, u32[]{:S(2)}) copy-start(f32[2048]{0:T(1024)} %param.15) | copy-start | bytes 24580

commit v4 on v3

--- a/solution.py
+++ b/solution.py
@@ -13,6 +13,7 @@
 MEMBERS = 6
 LANES = 128
 LOW = 256
+TILE = 512
 PARTS = 4
 CHUNKS = 4
 MESH = pl.DeviceIdType.MESH
@@ -296,18 +297,18 @@
 
     for c in range(CHUNKS):
         def tile(step, none):
-            at = pl.multiple_of(step * LOW, LOW)
-            cols = pl.ds(pl.multiple_of(c * chunk + step * LOW, LOW), LOW)
+            at = pl.multiple_of(step * TILE, TILE)
+            cols = pl.ds(pl.multiple_of(c * chunk + step * TILE, TILE), TILE)
             product = jnp.dot(lhs[...], dosage[:, cols], preferred_element_type=f32)
             mean = means[me, :, cols]
             for k in range(n_person):
                 rows = product[k * share : (k + 1) * share]
                 centred = rows - level[k * share : (k + 1) * share] * mean
-                partial[c, k, :, pl.ds(at, LOW)] = centred.astype(bf16)
+                partial[c, k, :, pl.ds(at, TILE)] = centred.astype(bf16)
                 own_part[k, :, cols] = rows
             return none
 
-        lax.fori_loop(0, chunk // LOW, tile, 0)
+        lax.fori_loop(0, chunk // TILE, tile, 0)
 
         def sum_source(peer):
             return partial.at[c, peer]

time: 37.4 us -> 37.3 us (level)
  no operation moved by 1% of the time
where the time goes in v4:
time: 37.3 us; the launch traced here: 37.1 us
  Pallas kernels  34.8 us (93%)
  other arithmetic  1.64 us (4%)
  between operations  0.69 us (2%)
    pallas_call x1, Pallas kernels, per_device(): pl.pallas_call(functools.partial(kernel, n_person, n_var), out_shape=jax....  34.8 us
    mul x1, other arithmetic, per_device(): (1 - strong_set).astype(f32)  1.64 us

profile of v4, /device:TPU:0, one launch (start us, length us, event | category | flops | bytes accessed | tf_op | source)
XLA Modules:
  0.0 37.1 jit_solution(4986665465130419067)
XLA Ops:
  0.6 0.0 copy-start
  0.6 0.0 copy-start.2
  0.7 0.0 copy-start.1
  0.7 34.8 %shard_map.104 = f32[16,2048]{1,0:T(8,128)} custom-call(f32[8,3072]{1,0:T(8,128)} %pred_ref.1, s32[1,3072]{1,0:T(1,128)} %bitcast.4, s32[1,3072]{1,0:T(1,128)} %bitcast.5, s32[1,3072]{1,0:T(1,128)} %bitcast.6, s32[1,3072]{1,0:T(1,128)} %bitcast.7, s32[512,2048]{1,0:T(8,128)} %geno_hbm.1), custom_call_target="tpu_custom_call" | custom-call | tf_op jit(solution)/shard_map/pallas_call | solution.py:365
  35.5 0.0 copy-done
  35.5 0.0 copy-done.2
  35.5 0.0 copy-done.1
  35.5 1.6 %maximum_multiply_fusion = (f32[16,2048]{1,0:T(8,128)}, f32[16,2048]{1,0:T(8,128)}) fusion(s32[16,2048]{1,0:T(8,128)S(1)} %copy-done, f32[16]{0:T(128)S(1)} %copy-done.2, f32[16,2048]{1,0:T(8,128)} %shard_map.104, f32[2048]{0:T(1024)S(1)} %copy-done.1), kind=kLoop, calls=%fused_computation | loop fusion | flops 262144 | bytes 532544 | tf_op jit(solution)/shard_map/mul | solution.py:409
Async XLA Ops:
  0.6 34.8 %copy-start = (s32[16,2048]{1,0:T(8,128)S(1)}, s32[16,2048]{1,0:T(8,128)}, u32[]{:S(2)}) copy-start(s32[16,2048]{1,0:T(8,128)} %param.17) | copy-start | bytes 393220
  0.6 34.8 %copy-start.2 = (f32[16]{0:T(128)S(1)}, f32[16]{0:T(128)}, u32[]{:S(2)}) copy-start(f32[16]{0:T(128)} %param.16) | copy-start | bytes 196
  0.7 34.8 %copy-start.1 = (f32[2048]{0:T(1024)S(1)}, f32[2048]{0:T(1024)}, u32[]{:S(2)}) copy-start(f32[2048]{0:T(1024)} %param.15) | copy-start | bytes 24580
